TPU v7x, 32 devices: a whole 2x2x4 slice. The times are simulated.
32 devices in a mesh: dp: 8 (over z, y), tensor: 4 (over x, core).
Axes of the slice: x: 2, y: 2, z: 4, core: 2. Of those that a mesh axis runs over, the one named last changes fastest.
Arguments:
- tokens: bfloat16 [8192, 2048], P(('dp', 'tensor')), may hold values from -6 to 6
- ln_gain: float32 [2048], replicated, may hold values from 0.1 to 1.9
- ln_bias: float32 [2048], replicated, may hold values from -1.75 to 1.75
- w_qkv: bfloat16 [2048, 3, 2048], P('dp', None, 'tensor'), may hold values from -0.125 to 0.125
- b_qkv: float32 [3, 2048], P(None, 'tensor'), may hold values from -3 to 3
- w_out: bfloat16 [2048, 2048], P('tensor', 'dp'), may hold values from -0.5 to 0.5
- w_up: bfloat16 [2048, 8192], P('dp', 'tensor'), may hold values from -0.125 to 0.125
- b_up: float32 [8192], P('tensor'), may hold values from -3 to 3
- w_down: bfloat16 [8192, 2048], P('tensor', 'dp'), may hold values from -0.0625 to 0.0625
- out_bias: float32 [2048], replicated, may hold values from -3 to 3
- cotangent: bfloat16 [8192, 2048], P(('dp', 'tensor')), may hold values from -12 to 12, as said below
Outputs:
- output: bfloat16 [8192, 2048], P(('dp', 'tensor'))
- grad_tokens: float32 [8192, 2048], P(('dp', 'tensor'))
- grad_ln_gain: float32 [2048], replicated
- grad_ln_bias: float32 [2048], replicated
- grad_w_qkv: float32 [2048, 3, 2048], P('dp', None, 'tensor')
- grad_b_qkv: float32 [3, 2048], P(None, 'tensor')
- grad_w_out: float32 [2048, 2048], P('tensor', 'dp')
- grad_w_up: float32 [2048, 8192], P('dp', 'tensor')
- grad_b_up: float32 [8192], P('tensor')
- grad_w_down: float32 [8192, 2048], P('tensor', 'dp')
- grad_out_bias: float32 [2048], replicated
Inputs may be any that keep to these rules, and one draw needn't show every extreme that they name: cotangent of the block's output.
All inputs are finite; a program needn't handle non-finite values.
Results may differ from a plain program's by a relative error of at most 0.012.
The roundings to bfloat16 on the way count: a program that leaves them out, or rounds other values in their place, can miss the bound.
Values may be sent and summed in bfloat16 or wider, within the bound.
A program may use at most 256 MiB of HBM per device.

v0:
```python
import functools
import math

import jax
import jax.numpy as jnp
import numpy as np
from jax import lax
from jax.experimental import pallas as pl
from jax.experimental.pallas import tpu as pltpu
from jax.sharding import PartitionSpec as P

HEAD_DIM = 64
ROT = 32
epsilon = 1e-05
big_negative = -1e30

f32 = jnp.float32
bf16 = jnp.bfloat16
NN = (((1,), (0,)), ((), ()))
NT = (((1,), (1,)), ((), ()))
TN = (((0,), (0,)), ((), ()))
dot = functools.partial(lax.dot_general, preferred_element_type=f32)

GELU_A = math.sqrt(2.0 / math.pi)
GELU_B = 0.044715
CHUNK = 512
Q_BLOCK = 128
LANES = 128


def gelu_both(h):
    square = h * h
    t = jnp.tanh(h * (GELU_A + (GELU_A * GELU_B) * square))
    half = 0.5 * (1.0 + t)
    slope = half + (0.5 * h) * (1.0 - t * t) * (GELU_A + (3.0 * GELU_A * GELU_B) * square)
    return h * half, slope


def rotary_tables(row_count):
    half_rot = ROT // 2
    positions = np.arange(row_count, dtype=np.float32)
    freqs = np.float32(10000.0) ** (-(2.0 * np.arange(half_rot, dtype=np.float32)) / np.float32(ROT))
    angles = positions[:, None] * freqs.astype(np.float32)[None, :]
    cosines, sines = np.cos(angles), np.sin(angles)
    rest = np.zeros((row_count, HEAD_DIM - ROT), np.float32)
    c_head = np.concatenate([cosines, cosines, rest + 1.0], axis=1)
    s_head = np.concatenate([-sines, sines, rest], axis=1)
    pair = lambda t: np.concatenate([t, t], axis=1).astype(np.float32)
    return pair(c_head), pair(s_head)


def rotate(field, cosines, sines):
    half = ROT // 2
    lane = lax.broadcasted_iota(jnp.int32, field.shape, 1)
    first = lax.rem(lane, HEAD_DIM) < half
    partner = jnp.where(
        first, pltpu.roll(field, LANES - half, 1), pltpu.roll(field, half, 1)
    )
    return field * cosines + partner * sines


ORDER = (
    "s:Glo", "ln", "s:Od", "s:Gx", "s:Nc", "s:Qc", "s:Oc", "r:Qg", "r:Og", "s:D0d", "s:U0e",
    "s:Nx", "s:U0d", "s:Nlo", "s:Qd", "r:Ncx", "s:U0c", "r:U0h", "r:Gxlo", "r:U0g", "s:U0a",
    "r:Nxlo", "r:Gcxlo", "s:Oe", "r:Oh", "s:Gc", "r:Gcx", "s:Qe", "r:U0f", "s:Oa", "r:Ncxlo",
    "s:Qa", "r:Of", "r:Qh", "hid00", "s:D0e", "r:Qf", "hid01", "near:D011", "s:D0a", "near:D030",
    "proj0", "s:D0c", "att00", "near:D031", "att01", "far:D00", "r:D0h", "r:D0f", "swap:D0",
    "r:D0g", "far:D01", "proj1", "att10", "att11", "near:A30", "core:o11", "core:o01", "cross:o1",
    "core:o10", "far:A0", "dh00", "near:A10", "dh01", "core:n11", "level:o", "near:U031",
    "cross:n1", "core:n10", "near:U010", "near:A31", "fin:A", "far:U01", "near:U030", "near:U011",
    "core:n01", "core:o00", "level:n", "cross:o0", "fin:U0", "near:A11", "far:A1", "cross:n0",
    "near:D010", "swap:U0", "far:U00", "core:n00", "own:o", "swap:A", "fin:D0", "own:n", "small",
)


def block_kernel(
    tokens, cot, gain, shift, out_bias, wq_in, wo_in, wu_in, wd_in, bq_in, bu_in, cos_t, sin_t,
    o_out, o_gt, o_vec, o_part, ry, rm, rl, rc, rx, rr_lo,
    XN, G, WU, WD, WQ, WO, ACT, DH, ATT, DP, KS, VS, DK, DV, YS, FF, RING, LD, VEC, SV, SR,
    ssem, rsem, lsem,
):
    T, D = tokens.shape
    R = wu_in.shape[0]
    F = wu_in.shape[1] // 2
    H = wo_in.shape[0] // 2
    ROWS = 8 * T
    LEN = 4 * T
    half_d = D // 2
    LN_ROWS = min(T, 64)

    dp = lax.axis_index("dp")
    tp = lax.axis_index("tensor")
    hi = lax.div(dp, 4)
    lo = lax.rem(lax.div(dp, 2), 2)
    y = lax.rem(dp, 2)
    x = lax.div(tp, 2)
    c = lax.rem(tp, 2)

    def device(hi_=hi, lo_=lo, y_=y, x_=x, c_=c):
        return {"dp": (hi_ * 2 + lo_) * 2 + y_, "tensor": x_ * 2 + c_}

    to_x = device(x_=1 - x)
    to_c = device(c_=1 - c)
    to_lo = device(lo_=1 - lo)
    to_y = device(y_=1 - y)
    to_hi = device(hi_=1 - hi)
    to_hilo = device(hi_=1 - hi, lo_=1 - lo)
    partners = [to_x, to_c, to_lo, to_y, to_hi, to_hilo]

    mult = pl.multiple_of

    n_copies = [0]
    n_local = [0]
    pending = []

    class Send:
        def __init__(self, src, dst, dev):
            i = n_copies[0]
            n_copies[0] += 1
            self.d = pltpu.make_async_remote_copy(
                src_ref=src, dst_ref=dst, send_sem=ssem.at[i], recv_sem=rsem.at[i],
                device_id=dev, device_id_type=pl.DeviceIdType.MESH,
            )
            self.open = False
            self.arrived = False

        def start(self):
            self.d.start()
            self.open = True
            pending.append(self)

        def got(self):
            if not self.arrived:
                self.d.wait_recv()
            self.arrived = True

        def done(self):
            if self.open:
                self.d.wait_send()
            self.open = False

    class Local:
        def __init__(self, src, dst):
            i = n_local[0]
            n_local[0] += 1
            self.d = pltpu.make_async_copy(src, dst, lsem.at[i])
            self.d.start()
            self.open = True

        def done(self):
            if self.open:
                self.d.wait()
            self.open = False

    sends = {}

    def got(*names):
        for n in names:
            sends[n].got()

    def start(*names):
        for n in names:
            sends[n].start()

    steps = {}

    def col(p, low):
        return mult(p * 2 * R + low * R, R)

    def abs_block(p, low):
        hi_ = hi if p < 2 else 1 - hi
        y_ = y if p % 2 == 0 else 1 - y
        return mult(((hi_ * 2 + low) * 2 + y_) * R, R)

    pieces = [(p, low) for p in range(4) for low in range(2)]

    def piece_cols(p, low):
        return slice(p * 2 * R + low * R, p * 2 * R + (low + 1) * R)

    def piece_ds(p, low):
        return pl.ds(p * 2 * R + low * R, R)

    def row(low, xx, cc):
        return mult((low * 4 + xx * 2 + cc) * T, T)

    own_row = row(lo, x, c)
    own_rows = pl.ds(own_row, T)

    tok_loads, cot_loads = [], []
    for p, low in pieces:
        src = pl.ds(abs_block(p, low), R)
        tok_loads.append(Local(tokens.at[:, src], RING.at[0, :, piece_ds(p, low)]))
    for p, low in pieces:
        src = pl.ds(abs_block(p, low), R)
        cot_loads.append(Local(cot.at[:, src], G.at[own_rows, piece_ds(p, low)]))

    own_weights = {}

    def weight(w, src, land):
        own_weights[w] = Local(src(lo), land(0, lo))
        sends[w + "a"] = Send(src(1 - lo), land(0, lo), to_lo)
        sends[w + "c"] = Send(src(lo), land(2, lo), to_hi)
        sends[w + "e"] = Send(src(1 - lo), land(2, lo), to_hilo)
        sends[w + "d"] = Send(src(lo), land(1, lo), to_y)
        sends[w + "f"] = Send(land(0, 1 - lo), land(1, 1 - lo), to_y)
        sends[w + "g"] = Send(land(2, lo), land(3, lo), to_y)
        sends[w + "h"] = Send(land(2, 1 - lo), land(3, 1 - lo), to_y)
        for n in "aced":
            steps["s:" + w + n] = functools.partial(start, w + n)
        for n, before in (("f", "a"), ("g", "c"), ("h", "e")):
            steps["r:" + w + n] = functools.partial(relay, w + before, w + n)

    def relay(before, *after):
        got(before)
        start(*after)

    def weight_ready(*ws):
        for w in ws:
            own_weights[w].done()
            got(w + "d", w + "f", w + "g", w + "h")

    weight(
        "U0",
        lambda h: wu_in.at[:, pl.ds(mult(h * F, F), F)],
        lambda p, low: WU.at[pl.ds(col(p, low), R), :],
    )
    weight(
        "Q",
        lambda h: wq_in.at[:, :, pl.ds(mult(h * H, H), H)],
        lambda p, low: WQ.at[:, pl.ds(col(p, low), R), :],
    )
    weight(
        "O",
        lambda h: wo_in.at[pl.ds(mult(h * H, H), H), :],
        lambda p, low: WO.at[:, pl.ds(col(p, low), R)],
    )
    weight(
        "D0",
        lambda h: wd_in.at[pl.ds(mult(h * F, F), F), :],
        lambda p, low: WD.at[:, pl.ds(col(p, low), R)],
    )

    def rows_over(r, buf):
        def at(low, xx):
            return buf.at[pl.ds(row(low, xx, c), T), :]

        sends[r + "lo"] = Send(at(lo, x), at(lo, x), to_lo)
        sends[r + "x"] = Send(at(lo, x), at(lo, x), to_x)
        sends[r + "xlo"] = Send(at(1 - lo, x), at(1 - lo, x), to_x)
        sends[r + "c"] = Send(at(lo, x), at(lo, x), to_c)
        sends[r + "clo"] = Send(at(1 - lo, x), at(1 - lo, x), to_c)
        sends[r + "cx"] = Send(at(lo, 1 - x), at(lo, 1 - x), to_c)
        sends[r + "cxlo"] = Send(at(1 - lo, 1 - x), at(1 - lo, 1 - x), to_c)
        steps["r:" + r + "xlo"] = functools.partial(relay, r + "lo", r + "xlo", r + "clo")
        steps["r:" + r + "cx"] = functools.partial(relay, r + "x", r + "cx")
        steps["r:" + r + "cxlo"] = functools.partial(relay, r + "xlo", r + "cxlo")

    rows_over("N", XN)
    rows_over("G", G)

    def rows_ready(*rs):
        for r in rs:
            got(r + "c", r + "clo", r + "cx", r + "cxlo")

    def start_g(n):
        for ld in cot_loads:
            ld.done()
        start("G" + n)

    for n in ("lo", "x", "c"):
        steps["s:N" + n] = functools.partial(start, "N" + n)
        steps["s:G" + n] = functools.partial(start_g, n)

    def normalise(k, sub):
        activ = RING[k, sub, :].astype(f32)
        average = jnp.mean(activ, axis=1, keepdims=True)
        centered = activ - average
        variance = jnp.mean(centered * centered, axis=1, keepdims=True)
        inv_std = lax.rsqrt(variance + epsilon)
        return centered * inv_std, inv_std

    def sub_rows(i):
        return pl.ds(mult(i * LN_ROWS, LN_ROWS), LN_ROWS)

    def step_ln():
        for p, low in pieces:
            src = pl.ds(abs_block(p, low), R)
            VEC[0:1, piece_ds(p, low)] = gain[:, src]
            VEC[1:2, piece_ds(p, low)] = shift[:, src]
            VEC[2:3, piece_ds(p, low)] = out_bias[:, src]
        for ld in tok_loads:
            ld.done()

        def body(i, _):
            x_hat, _unused = normalise(0, sub_rows(i))
            XN[pl.ds(mult(own_row + i * LN_ROWS, LN_ROWS), LN_ROWS), :] = (
                x_hat * VEC[0:1, :] + VEC[1:2, :]
            ).astype(bf16)

        lax.fori_loop(0, T // LN_ROWS, body, None)

    steps["ln"] = step_ln

    def tiles(first, stop, body):
        lax.fori_loop(first, stop, lambda i, _: body(pl.ds(mult(i * T, T), T)), None)

    def step_hid(first, stop):
        weight_ready("U0")
        rows_ready("N")

        def body(rows):
            xn = XN[rows, :]
            for m in range(0, F, R):
                cols = slice(m, m + R)
                bias = bu_in[:, pl.ds(mult(lo * F + m, R), R)]
                h = dot(xn, WU[:, cols], NN) + bias
                act, slope = gelu_both(h)
                ACT[rows, cols] = act.astype(bf16)
                DH[rows, cols] = slope.astype(bf16)

        tiles(first, stop, body)

    steps["hid00"] = functools.partial(step_hid, 0, 4)
    steps["hid01"] = functools.partial(step_hid, 4, 8)

    def step_dh(first, stop):
        weight_ready("D0")
        rows_ready("G")
        if first == 0:
            VEC[3:4, 0:F] = jnp.zeros((1, F), f32)

        def body(rows):
            gg = G[rows, :]
            for m in range(0, F, R):
                cols = slice(m, m + R)
                dh = (dot(gg, WD[cols, :], NT) * DH[rows, cols].astype(f32)).astype(bf16)
                DH[rows, cols] = dh
                VEC[3:4, cols] += jnp.sum(dh.astype(f32), axis=0, keepdims=True)

        tiles(first, stop, body)

    steps["dh00"] = functools.partial(step_dh, 0, 4)
    steps["dh01"] = functools.partial(step_dh, 4, 8)

    Q, DA = 0, 1

    def seq_row(s, off):
        return mult((1 - lo if s == 0 else lo) * LEN + off, Q_BLOCK)

    def head_rows(which, begin, cc):
        cols = pl.ds(mult(begin // T * H + cc, LANES), LANES)
        return YS[1, which, begin % T : begin % T + Q_BLOCK, cols]

    def step_proj(s):
        weight_ready("Q", "O")
        rows_ready("N", "G")

        def body(i, _):
            pos = pl.ds(mult(i * T, T), T)
            rows = pl.ds(mult(seq_row(s, 0) + i * T, T), T)
            cs, sn = cos_t[pos, :], sin_t[pos, :]

            def turned(v):
                return [
                    rotate(v[:, a : a + LANES], cs, sn).astype(bf16) for a in range(0, H, LANES)
                ]

            def put(which, vs):
                for n, u in enumerate(vs):
                    YS[1, which, :, pl.ds(mult(i * H + n * LANES, LANES), LANES)] = u

            xn = XN[rows, :]

            def part(k):
                return dot(xn, WQ[k], NN) + bq_in[k : k + 1, pl.ds(mult(lo * H, LANES), H)]

            put(Q, turned(part(0)))
            for n, u in enumerate(turned(part(1))):
                KS[pos, n * LANES : (n + 1) * LANES] = u
            VS[pos, :] = part(2).astype(bf16)
            d_att = dot(G[rows, :], WO[...], NT).astype(bf16)
            put(DA, [d_att[:, a : a + LANES] for a in range(0, H, LANES)])

        lax.fori_loop(0, 4, body, None)

    def step_att(s, first_pair, n_pairs):
        first = lax.broadcasted_iota(jnp.int32, (Q_BLOCK, LANES), 1) < HEAD_DIM
        scaling = HEAD_DIM**-0.5

        def split(v):
            zero = jnp.zeros_like(v)
            return jnp.concatenate([jnp.where(first, v, zero), jnp.where(first, zero, v)], axis=0)

        def join(v):
            return jnp.where(first, v[:Q_BLOCK], v[Q_BLOCK:])

        def pair(hp, _):
            cc = hp * LANES
            out_cols = pl.ds(mult(cc, LANES), LANES)
            for i in range(LEN // Q_BLOCK):
                rr = pl.ds(i * Q_BLOCK, Q_BLOCK)
                out_rows = pl.ds(seq_row(s, i * Q_BLOCK), Q_BLOCK)
                n = (i + 1) * Q_BLOCK
                old = n - Q_BLOCK
                qm = split(head_rows(Q, old, cc))
                dm = split(head_rows(DA, old, cc))
                kk = KS[0:n, out_cols]
                vv = VS[0:n, out_cols]
                st = dot(kk, qm * jnp.asarray(scaling, bf16), NT)
                kpos = lax.broadcasted_iota(jnp.int32, (Q_BLOCK, 2 * Q_BLOCK), 0)
                qpos = lax.broadcasted_iota(jnp.int32, (Q_BLOCK, 2 * Q_BLOCK), 1)
                qpos = jnp.where(qpos < Q_BLOCK, qpos, qpos - Q_BLOCK)
                diagonal = jnp.where(kpos <= qpos, st[old:], big_negative)
                st = diagonal if i == 0 else jnp.concatenate([st[:old], diagonal], axis=0)
                ex = jnp.exp(st - jnp.max(st, axis=0, keepdims=True))
                prob = ex * (1.0 / jnp.sum(ex, axis=0, keepdims=True))
                pb = prob.astype(bf16)
                ATT[out_rows, out_cols] = join(dot(pb, vv, TN)).astype(bf16)
                dv = dot(pb, dm, NN)
                dprob = dot(vv, dm * jnp.asarray(scaling, bf16), NT)
                centre = jnp.sum(dprob * prob, axis=0, keepdims=True)
                ds = (prob * (dprob - centre)).astype(bf16)
                dq = join(dot(ds, kk, TN))
                DP[out_rows, out_cols] = rotate(dq, cos_t[rr, :], -sin_t[rr, :]).astype(bf16)
                dk = dot(ds, qm, NN)
                if i > 0:
                    DK[0:old, :] += dk[:old]
                    DV[0:old, :] += dv[:old]
                DK[rr, :] = dk[old:]
                DV[rr, :] = dv[old:]
            seq = pl.ds(seq_row(s, 0), LEN)
            DP[seq, pl.ds(mult(H + cc, LANES), LANES)] = rotate(
                DK[...], cos_t[...], -sin_t[...]
            ).astype(bf16)
            DP[seq, pl.ds(mult(2 * H + cc, LANES), LANES)] = DV[...].astype(bf16)

        lax.fori_loop(first_pair, first_pair + n_pairs, pair, None)

    half_pairs = H // LANES // 2
    for s in range(2):
        steps["proj%d" % s] = functools.partial(step_proj, s)
        if half_pairs:
            steps["att%d0" % s] = functools.partial(step_att, s, 0, half_pairs)
            steps["att%d1" % s] = functools.partial(step_att, s, half_pairs, half_pairs)
            steps["att%d" % s] = functools.partial(step_att, s, 0, 2 * half_pairs)
        else:
            steps["att%d0" % s] = functools.partial(step_att, s, 0, 1)
            steps["att%d1" % s] = lambda: None
            steps["att%d" % s] = steps["att%d0" % s]

    ff_use = {0: [], 1: []}

    def ff_free(*which):
        for k in which:
            for ld in ff_use[k]:
                ld.done()
            ff_use[k] = []

    def cols_of(p, q):
        return pl.ds(col(p, lo if q == 0 else 1 - lo), R)

    def block_dn(p, q):
        gg = G[:, cols_of(p, q)]
        return [(m, dot(ACT[:, m : m + R], gg, TN)) for m in range(0, F, R)]

    def block_up(p, q):
        return [(0, dot(XN[:, cols_of(p, q)], DH[...], TN))]

    def block_at(p, q):
        cc = cols_of(p, q)
        return [(0, dot(XN[:, cc], DP[...], TN)), (3 * H, dot(ATT[...], G[:, cc], TN))]

    def weight_grad(g, i, block, needs):
        def slot(p, q):
            return (0 if p >= 2 else 2) + (1 - q)

        def pq(p, q):
            return "%d%d" % (p, q)

        for p, q in ((3, 1), (3, 0), (1, 1), (1, 0)):
            k = slot(p, q)
            sends["y" + g + pq(p, q)] = Send(YS.at[i, k], ry.at[i, k], to_y)
        sends["m" + g + "0"] = Send(YS.at[i, slot(3, 0)], rm.at[i, 0], to_hi)
        sends["m" + g + "1"] = Send(YS.at[i, slot(3, 1)], rm.at[i, 1], to_hilo)
        sends["l" + g] = Send(YS.at[i, slot(1, 1)], rl.at[i], to_lo)

        def near(p, q):
            needs()
            k = slot(p, q)
            for off, v in block(p, q):
                YS[i, k, :, off : off + v.shape[1]] = v.astype(bf16)
            start("y" + g + pq(p, q))

        def pass_on(p, q, then):
            k = slot(p, q)
            came = "y" + g + pq(p + 1, q)
            got(came)
            load = Local(ry.at[i, k], LD.at[0, 0:R, 0:F])
            vals = block(p, q)
            sends[came].done()
            load.done()
            for off, v in vals:
                cols = slice(off, off + v.shape[1])
                YS[i, k, :, cols] = (v + LD[0, 0:R, cols].astype(f32)).astype(bf16)
            start(then)

        def fin():
            ff_free(0)
            got("y" + g + "10")
            load = Local(ry.at[i, slot(0, 0)], LD.at[0, 0:R, 0:F])
            vals = block(0, 0)
            load.done()
            for off, v in vals:
                cols = slice(off, off + v.shape[1])
                FF[0, :, cols] = v + LD[0, 0:R, cols].astype(f32)
            ff_use[0] = [Local(FF.at[0], o_part.at[i])]

        for p, q in ((3, 1), (3, 0), (1, 1), (1, 0)):
            steps["near:" + g + pq(p, q)] = functools.partial(near, p, q)
        for q in range(2):
            steps["far:" + g + str(q)] = functools.partial(pass_on, 2, q, "m" + g + str(q))
        steps["swap:" + g] = functools.partial(pass_on, 0, 1, "l" + g)
        steps["fin:" + g] = fin

    weight_grad("D0", 0, block_dn, lambda: rows_ready("G"))
    weight_grad("A", 1, block_at, lambda: None)
    weight_grad("U0", 2, block_up, lambda: None)

    def rows_out(rr, cc):
        return dot(ACT[rr, :], WD[:, cc], NN) + dot(ATT[rr, :], WO[:, cc], NN)

    def rows_dn(rr, cc):
        v = dot(DH[rr, :], WU[cc, :], NT)
        for k in range(3):
            v = v + dot(DP[rr, k * H : (k + 1) * H], WQ[k, cc, :], NT)
        return v

    ring_use = {0: None, 1: None, 2: None}
    ring_next = [0]

    def ring_slot():
        k = ring_next[0]
        ring_next[0] = (k + 1) % 3
        if ring_use[k] is not None:
            ring_use[k].done()
            ring_use[k] = None
        return k

    def load_tokens():
        k = ring_slot()
        return k, [
            Local(tokens.at[:, pl.ds(abs_block(p, low), R)], RING.at[k, :, piece_ds(p, low)])
            for p, low in pieces
        ]

    def own_sub(sub):
        return jnp.concatenate([FF[0, sub, :], FF[1, sub, :]], axis=1) + LD[0, sub, :].astype(f32)

    def finish_out(k_tok):
        k = ring_slot()

        def body(i, _):
            sub = sub_rows(i)
            RING[k, sub, :] = (
                RING[k_tok, sub, :].astype(f32) + own_sub(sub) + VEC[2:3, :]
            ).astype(bf16)

        lax.fori_loop(0, T // LN_ROWS, body, None)
        stores = [
            Local(RING.at[k, :, piece_ds(p, low)], o_out.at[:, pl.ds(abs_block(p, low), R)])
            for p, low in pieces
        ]
        for st in stores:
            st.done()

    def finish_dn(k_tok):
        VEC[4:6, :] = jnp.zeros((2, D), f32)

        def body(i, _):
            sub = sub_rows(i)
            x_hat, inv_std = normalise(k_tok, sub)
            dn = own_sub(sub)
            VEC[4:5, :] += jnp.sum(dn * x_hat, axis=0, keepdims=True)
            VEC[5:6, :] += jnp.sum(dn, axis=0, keepdims=True)
            scaled = dn * VEC[0:1, :]
            gt = (
                inv_std
                * (
                    scaled
                    - jnp.mean(scaled, axis=1, keepdims=True)
                    - x_hat * jnp.mean(scaled * x_hat, axis=1, keepdims=True)
                )
                + G[pl.ds(mult(own_row + i * LN_ROWS, LN_ROWS), LN_ROWS), :].astype(f32)
            )
            FF[0, sub, :] = gt[:, :half_d]
            FF[1, sub, :] = gt[:, half_d:]

        lax.fori_loop(0, T // LN_ROWS, body, None)
        for p, low in pieces:
            dst = pl.ds(abs_block(p, low), R)
            src = pl.ds((p % 2) * 2 * R + low * R, R)
            ff_use[p // 2].append(Local(FF.at[p // 2, :, src], o_gt.at[:, dst]))

    def owners(w, i, partial, needs, finish):
        def chunks(low, xx, cc, loads, store):
            rr = pl.ds(row(low, xx, cc), T)
            for ld in loads:
                ld.done()

            def body(j, _):
                cols = pl.ds(mult(j * CHUNK, CHUNK), CHUNK)
                v = partial(rr, cols)
                for k in range(len(loads)):
                    v = v + LD[k, :, cols].astype(f32)
                store(j, cols, v)

            lax.fori_loop(0, D // CHUNK, body, None)

        def put(name, low, xx, cc, srcs, dst, dev):
            needs()
            loads = [Local(src, LD.at[k]) for k, src in enumerate(srcs)]
            k = ring_slot()

            def store(j, cols, v):
                RING[k, :, cols] = v.astype(bf16)

            chunks(low, xx, cc, loads, store)
            sends[name] = Send(RING.at[k], dst, dev)
            start(name)
            ring_use[k] = sends[name]

        def core(dlo, dx):
            low = lo if dlo == 0 else 1 - lo
            xx = x if dx == 0 else 1 - x
            name = "c%s%d%d" % (w, dlo, dx)
            put(name, low, xx, 1 - c, [], rc.at[i, 2 * dlo + dx], to_c)

        def cross(dlo):
            low = lo if dlo == 0 else 1 - lo
            got("c%s%d1" % (w, dlo))
            name = "x%s%d" % (w, dlo)
            put(name, low, 1 - x, c, [rc.at[i, 2 * dlo + 1]], rx.at[i, dlo], to_x)

        def level():
            got("c%s10" % w, "x%s1" % w)
            put("l" + w, 1 - lo, x, c, [rc.at[i, 2], rx.at[i, 1]], rr_lo.at[i], to_lo)

        def own():
            k_tok, tok_ld = load_tokens()
            got("c%s00" % w, "x%s0" % w)
            loads = [Local(rc.at[i, 0], LD.at[0]), Local(rx.at[i, 0], LD.at[1])]
            ff_free(0, 1)
            n = D // CHUNK // 2

            def store(j, cols, v):
                part = pl.ds(mult(lax.rem(j, n) * CHUNK, CHUNK), CHUNK)
                FF[lax.div(j, n), :, part] = v

            chunks(lo, x, c, loads, store)
            got("l" + w)
            Local(rr_lo.at[i], LD.at[0]).done()
            for ld in tok_ld:
                ld.done()
            finish(k_tok)

        for dlo in range(2):
            for dx in range(2):
                steps["core:%s%d%d" % (w, dlo, dx)] = functools.partial(core, dlo, dx)
            steps["cross:%s%d" % (w, dlo)] = functools.partial(cross, dlo)
        steps["level:" + w] = level
        steps["own:" + w] = own

    owners("o", 0, rows_out, lambda: weight_ready("D0"), finish_out)
    owners("n", 1, rows_dn, lambda: None, finish_dn)

    def step_small():
        SV[...] = jnp.zeros_like(SV)
        VEC[6:7, 0 : 3 * H] = jnp.zeros((1, 3 * H), f32)
        VEC[7:8, :] = jnp.zeros((1, D), f32)

        def body(rows):
            VEC[6:7, 0 : 3 * H] += jnp.sum(DP[rows, :].astype(f32), axis=0, keepdims=True)

        tiles(0, ROWS // T, body)

        def g_body(i, _):
            rows = pl.ds(mult(own_row + i * LN_ROWS, LN_ROWS), LN_ROWS)
            VEC[7:8, :] += jnp.sum(G[rows, :].astype(f32), axis=0, keepdims=True)

        lax.fori_loop(0, T // LN_ROWS, g_body, None)
        for p, low in pieces:
            dst = pl.ds(abs_block(p, low), R)
            SV[0:2, dst] = VEC[4:6, piece_cols(p, low)]
            SV[2:3, dst] = VEC[7:8, piece_cols(p, low)]
        SV[3:4, pl.ds(mult(lo * F, F), F)] = VEC[3:4, 0:F]
        for k in range(3):
            SV[4 + k : 5 + k, pl.ds(mult(lo * H, LANES), H)] = VEC[6:7, k * H : (k + 1) * H]
        for k, dev in enumerate((to_y, to_hi, to_lo, to_x, to_c)):
            s = Send(SV, SR.at[k], dev)
            s.start()
            s.got()
            s.done()
            if k < 3:
                SV[...] += SR[k]
            else:
                SV[0:3, :] += SR[k, 0:3, :]
        o_vec[...] = SV[...]

    steps["small"] = step_small

    barrier = pltpu.get_barrier_semaphore()
    for dev in partners:
        pl.semaphore_signal(barrier, inc=1, device_id=dev, device_id_type=pl.DeviceIdType.MESH)
    pl.semaphore_wait(barrier, len(partners))
    for name in ORDER:
        steps[name]()
    ff_free(0, 1)
    for s in pending:
        s.got()
        s.done()
    assert n_copies[0] <= ssem.shape[0] and n_local[0] <= lsem.shape[0], (n_copies, n_local)


def finish_kernel(
    b_out, b_gt, b_vec, b_part, rm, rl,
    o_out, o_gt, o_gain, o_shift, o_bias, o_bu, o_bq, o_gq, o_go, o_gu, o_gd,
    PART, RM, RL, OUT, GT, GU, GD, GQ, GO, lsem,
):
    R, F = PART.shape[1:]
    H = o_go.shape[0] // 2
    lo = lax.rem(lax.div(lax.axis_index("dp"), 2), 2)
    mult = pl.multiple_of
    n = [0]

    def copy(src, dst):
        d = pltpu.make_async_copy(src, dst, lsem.at[n[0]])
        n[0] += 1
        d.start()
        return d

    order = (1, 0, 2)
    loads = {i: [copy(b_part.at[i], PART.at[i]), copy(rm.at[i], RM.at[i]), copy(rl.at[i], RL.at[i])] for i in order}
    load_out = copy(b_out, OUT)
    load_gt = copy(b_gt, GT)
    o_gain[...] = b_vec[0:1, :]
    o_shift[...] = b_vec[1:2, :]
    o_bias[...] = b_vec[2:3, :]
    o_bu[...] = b_vec[3:4, 0 : 2 * F]
    o_bq[...] = b_vec[4:7, 0 : 2 * H]
    stores = []

    def halves(i, put):
        for ld in loads[i]:
            ld.wait()
        for m in range(0, F, R):
            cols = slice(m, m + R)
            put(lo, m, PART[i, :, cols] + RM[i, 0, :, cols].astype(f32))
            put(1 - lo, m, RL[i, :, cols].astype(f32) + RM[i, 1, :, cols].astype(f32))

    def put_at(half, m, v):
        if m < 3 * H:
            GQ[m // H, :, pl.ds(mult(half * H, H), H)] = v
        else:
            GO[pl.ds(mult(half * H, H), H), :] = v

    def put_dn(half, m, v):
        GD[pl.ds(mult(half * F + m, R), R), :] = v

    def put_up(half, m, v):
        GU[:, pl.ds(mult(half * F + m, R), R)] = v

    for i, put, pairs in (
        (1, put_at, ((GQ, o_gq), (GO, o_go))), (0, put_dn, ((GD, o_gd),)), (2, put_up, ((GU, o_gu),)),
    ):
        halves(i, put)
        for src, dst in pairs:
            stores.append(copy(src, dst))
    load_out.wait()
    stores.append(copy(OUT, o_out))
    load_gt.wait()
    stores.append(copy(GT, o_gt))
    for st in stores:
        st.wait()


VMEM_LIMIT = 64 << 20


def fast_shards(tokens, ln_gain, ln_bias, w_qkv, b_qkv, w_out, w_up, b_up, w_down, out_bias, cot):
    T, D = tokens.shape
    R, F = w_up.shape[0], w_up.shape[1] // 2
    H = w_out.shape[0] // 2
    cos_t, sin_t = rotary_tables(4 * T)
    S = jax.ShapeDtypeStruct
    hbm = pl.BlockSpec(memory_space=pl.ANY)
    vm = pl.BlockSpec(memory_space=pltpu.VMEM)
    outs = pl.pallas_call(
        block_kernel,
        out_shape=(
            S((T, D), bf16), S((T, D), f32), S((8, D), f32), S((3, R, F), f32),
            S((3, 4, R, F), bf16), S((3, 2, R, F), bf16), S((3, R, F), bf16),
            S((2, 4, T, D), bf16), S((2, 2, T, D), bf16), S((2, T, D), bf16),
        ),
        in_specs=[hbm, hbm, vm, vm, vm, hbm, hbm, hbm, hbm, vm, vm, vm, vm],
        out_specs=(hbm, hbm, vm) + (hbm,) * 7,
        scratch_shapes=[
            pltpu.VMEM((8 * T, D), bf16),
            pltpu.VMEM((8 * T, D), bf16),
            pltpu.VMEM((D, F), bf16),
            pltpu.VMEM((F, D), bf16),
            pltpu.VMEM((3, D, H), bf16),
            pltpu.VMEM((H, D), bf16),
            pltpu.VMEM((8 * T, F), bf16),
            pltpu.VMEM((8 * T, F), bf16),
            pltpu.VMEM((8 * T, H), bf16),
            pltpu.VMEM((8 * T, 3 * H), bf16),
            pltpu.VMEM((4 * T, H), bf16),
            pltpu.VMEM((4 * T, H), bf16),
            pltpu.VMEM((4 * T, LANES), f32),
            pltpu.VMEM((4 * T, LANES), f32),
            pltpu.VMEM((3, 4, R, F), bf16),
            pltpu.VMEM((2, R, F), f32),
            pltpu.VMEM((3, T, D), bf16),
            pltpu.VMEM((2, T, D), bf16),
            pltpu.VMEM((8, D), f32),
            pltpu.VMEM((8, D), f32),
            pltpu.VMEM((5, 8, D), f32),
            pltpu.SemaphoreType.DMA((90,)),
            pltpu.SemaphoreType.DMA((90,)),
            pltpu.SemaphoreType.DMA((110,)),
        ],
        compiler_params=pltpu.CompilerParams(
            collective_id=0, has_side_effects=True, vmem_limit_bytes=VMEM_LIMIT
        ),
        name="parallel_block",
    )(
        tokens, cot, ln_gain.reshape(1, D), ln_bias.reshape(1, D), out_bias.reshape(1, D),
        w_qkv.transpose(1, 0, 2), w_out, w_up, w_down, b_qkv, b_up.reshape(1, 2 * F), cos_t, sin_t,
    )
    b_out, b_gt, b_vec, b_part, _, rm, rl = outs[:7]
    done = pl.pallas_call(
        finish_kernel,
        out_shape=(
            S((T, D), bf16), S((T, D), f32), S((1, D), f32), S((1, D), f32), S((1, D), f32),
            S((1, 2 * F), f32), S((3, 2 * H), f32),
            S((3, R, 2 * H), f32), S((2 * H, R), f32), S((R, 2 * F), f32), S((2 * F, R), f32),
        ),
        in_specs=[hbm, hbm, vm, hbm, hbm, hbm],
        out_specs=(hbm, hbm) + (vm,) * 5 + (hbm,) * 4,
        scratch_shapes=[
            pltpu.VMEM((3, R, F), f32),
            pltpu.VMEM((3, 2, R, F), bf16),
            pltpu.VMEM((3, R, F), bf16),
            pltpu.VMEM((T, D), bf16),
            pltpu.VMEM((T, D), f32),
            pltpu.VMEM((R, 2 * F), f32),
            pltpu.VMEM((2 * F, R), f32),
            pltpu.VMEM((3, R, 2 * H), f32),
            pltpu.VMEM((2 * H, R), f32),
            pltpu.SemaphoreType.DMA((20,)),
        ],
        compiler_params=pltpu.CompilerParams(vmem_limit_bytes=VMEM_LIMIT),
        name="finish",
    )(b_out, b_gt, b_vec, b_part, rm, rl)
    o_out, o_gt, o_gain, o_shift, o_bias, o_bu, o_bq, o_gq, o_go, o_gu, o_gd = done
    return (
        o_out, o_gt, o_gain.reshape(D), o_shift.reshape(D), o_gq.transpose(1, 0, 2), o_bq, o_go,
        o_gu, o_bu.reshape(2 * F), o_gd, o_bias.reshape(D),
    )


def plain_tables(row_count):
    half_rot = ROT // 2
    positions = jnp.arange(row_count).astype(jnp.float32)
    freqs = 10000.0 ** (-(2.0 * jnp.arange(half_rot).astype(jnp.float32)) / ROT)
    angles = positions[:, None] * freqs[None, :]
    return (jnp.cos(angles)[:, None, :], jnp.sin(angles)[:, None, :])


def plain_rotate(field, cosines, sines):
    half_rot = ROT // 2
    first = field[..., :half_rot]
    second = field[..., half_rot:ROT]
    return jnp.concatenate(
        [first * cosines - second * sines, second * cosines + first * sines, field[..., ROT:]],
        axis=-1,
    )


def gelu_tanh(values):
    return jax.nn.gelu(values, approximate=True)


def causal_scores(query_block, key_rows, block_index):
    block_len = query_block.shape[0]
    query_pos = block_index * block_len + jnp.arange(block_len)
    key_pos = jnp.arange(key_rows.shape[0])
    raw = jnp.einsum("qhd,khd->hqk", query_block, key_rows, preferred_element_type=jnp.float32)
    scaled = raw * HEAD_DIM ** (-0.5)
    return jnp.where(key_pos[None, None, :] <= query_pos[None, :, None], scaled, big_negative)


def attend_forward(queries, key_rows, value_rows, block_len):
    row_count, heads_here, head_size = queries.shape
    n_blocks = row_count // block_len
    query_blocks = queries.reshape(n_blocks, block_len, heads_here, head_size)

    def one_block(item):
        query_block, block_index = item
        scores = causal_scores(query_block, key_rows, block_index)
        top_score = jnp.max(scores, axis=2, keepdims=True)
        exponent = jnp.exp(scores - top_score)
        totals = jnp.sum(exponent, axis=2, keepdims=True)
        probability = (exponent / totals).astype(jnp.bfloat16)
        attended = jnp.einsum(
            "hqk,khd->qhd", probability, value_rows, preferred_element_type=jnp.float32
        )
        return (attended, (top_score + jnp.log(totals))[:, :, 0])

    attended, logsum = lax.map(one_block, (query_blocks, jnp.arange(n_blocks)))
    return (attended.reshape(row_count, heads_here * head_size), logsum)


def attend_backward(queries, key_rows, value_rows, grad_att, logsum, block_len):
    row_count, heads_here, head_size = queries.shape
    n_blocks = row_count // block_len
    query_blocks = queries.reshape(n_blocks, block_len, heads_here, head_size)
    grad_blocks = grad_att.reshape(n_blocks, block_len, heads_here, head_size)
    scaling = HEAD_DIM ** (-0.5)

    def one_block(carry, item):
        grad_keys, grad_values = carry
        query_block, grad_block, lse_block, block_index = item
        scores = causal_scores(query_block, key_rows, block_index)
        probability = jnp.exp(scores - lse_block[:, :, None])
        grad_probs = jnp.einsum(
            "qhd,khd->hqk", grad_block, value_rows, preferred_element_type=jnp.float32
        )
        centre = jnp.sum(grad_probs * probability, axis=2, keepdims=True)
        grad_scores = (probability * (grad_probs - centre) * scaling).astype(jnp.bfloat16)
        grad_query = jnp.einsum(
            "hqk,khd->qhd", grad_scores, key_rows, preferred_element_type=jnp.float32
        )
        grad_keys = grad_keys + jnp.einsum(
            "hqk,qhd->khd", grad_scores, query_block, preferred_element_type=jnp.float32
        )
        grad_values = grad_values + jnp.einsum(
            "hqk,qhd->khd",
            probability.astype(jnp.bfloat16),
            grad_block,
            preferred_element_type=jnp.float32,
        )
        return ((grad_keys, grad_values), grad_query)

    zero_rows = jnp.zeros(key_rows.shape, jnp.float32)
    (grad_keys, grad_values), grad_queries = lax.scan(
        one_block, (zero_rows, zero_rows), (query_blocks, grad_blocks, logsum, jnp.arange(n_blocks))
    )
    return (grad_queries.reshape(row_count, heads_here, head_size), grad_keys, grad_values)


def plain_shards(tokens, ln_gain, ln_bias, w_qkv, b_qkv, w_out, w_up, b_up, w_down, out_bias, cotangent):
    activ = tokens.astype(jnp.float32)
    average = jnp.mean(activ, axis=1, keepdims=True)
    centered = activ - average
    variance = jnp.mean(centered * centered, axis=1, keepdims=True)
    inv_std = lax.rsqrt(variance + epsilon)
    x_hat = centered * inv_std
    normed = lax.all_gather(
        (x_hat * ln_gain + ln_bias).astype(jnp.bfloat16), "tensor", axis=0, tiled=True
    )
    row_count = normed.shape[0]
    block_len = min(row_count, 512)
    qkv_full, out_full, up_full, down_full = (
        lax.all_gather(w_qkv, "dp", axis=0, tiled=True),
        lax.all_gather(w_out, "dp", axis=1, tiled=True),
        lax.all_gather(w_up, "dp", axis=0, tiled=True),
        lax.all_gather(w_down, "dp", axis=1, tiled=True),
    )
    heads_here = w_qkv.shape[2] // HEAD_DIM
    local_width = heads_here * HEAD_DIM
    head_shape = (row_count, heads_here, HEAD_DIM)
    project = (
        jnp.einsum("td,dcf->tcf", normed, qkv_full, preferred_element_type=jnp.float32) + b_qkv
    )
    cosines, sines = plain_tables(row_count)
    queries = plain_rotate(project[:, 0].reshape(head_shape), cosines, sines).astype(jnp.bfloat16)
    key_rows = plain_rotate(project[:, 1].reshape(head_shape), cosines, sines).astype(jnp.bfloat16)
    value_rows = project[:, 2].reshape(head_shape).astype(jnp.bfloat16)
    attended, logsum = attend_forward(queries, key_rows, value_rows, block_len)
    attended = attended.astype(jnp.bfloat16)
    hidden = jnp.dot(normed, up_full, preferred_element_type=jnp.float32) + b_up
    activated = gelu_tanh(hidden).astype(jnp.bfloat16)
    partial_rows = jnp.dot(attended, out_full, preferred_element_type=jnp.float32) + jnp.dot(
        activated, down_full, preferred_element_type=jnp.float32
    )
    summed = lax.psum_scatter(partial_rows, "tensor", scatter_dimension=0, tiled=True)
    output = (activ + summed + out_bias).astype(jnp.bfloat16)
    grad_local = cotangent.astype(jnp.float32)
    grad_rows = lax.all_gather(cotangent, "tensor", axis=0, tiled=True)
    grad_down = jnp.einsum("tf,td->fd", activated, grad_rows, preferred_element_type=jnp.float32)
    grad_act = jnp.einsum("td,fd->tf", grad_rows, down_full, preferred_element_type=jnp.float32)
    gelu_pull = jax.vjp(gelu_tanh, hidden)[1]
    grad_hidden = gelu_pull(grad_act)[0].astype(jnp.bfloat16)
    grad_up = jnp.einsum("td,tf->df", normed, grad_hidden, preferred_element_type=jnp.float32)
    grad_b_up = jnp.sum(grad_hidden.astype(jnp.float32), axis=0)
    grad_normed = jnp.einsum("tf,df->td", grad_hidden, up_full, preferred_element_type=jnp.float32)
    grad_out = jnp.einsum("tf,td->fd", attended, grad_rows, preferred_element_type=jnp.float32)
    grad_att = jnp.einsum(
        "td,fd->tf", grad_rows, out_full, preferred_element_type=jnp.float32
    ).astype(jnp.bfloat16)
    grad_queries, grad_keys, grad_values = attend_backward(
        queries, key_rows, value_rows, grad_att.reshape(head_shape), logsum, block_len
    )
    grad_q_pre = plain_rotate(grad_queries, cosines, -sines).reshape(row_count, local_width)
    grad_k_pre = plain_rotate(grad_keys, cosines, -sines).reshape(row_count, local_width)
    grad_project = jnp.stack(
        [grad_q_pre, grad_k_pre, grad_values.reshape(row_count, local_width)], axis=1
    ).astype(jnp.bfloat16)
    grad_qkv = jnp.einsum("td,tcf->dcf", normed, grad_project, preferred_element_type=jnp.float32)
    grad_b_qkv = jnp.sum(grad_project.astype(jnp.float32), axis=0)
    grad_normed = grad_normed + jnp.einsum(
        "tcf,dcf->td", grad_project, qkv_full, preferred_element_type=jnp.float32
    )
    grad_ln_out = lax.psum_scatter(grad_normed, "tensor", scatter_dimension=0, tiled=True)
    qkv_summed, out_summed, up_summed, down_summed = (
        lax.psum_scatter(grad_qkv, "dp", scatter_dimension=0, tiled=True),
        lax.psum_scatter(grad_out, "dp", scatter_dimension=1, tiled=True),
        lax.psum_scatter(grad_up, "dp", scatter_dimension=0, tiled=True),
        lax.psum_scatter(grad_down, "dp", scatter_dimension=1, tiled=True),
    )
    scaled_grad = grad_ln_out * ln_gain
    grad_tokens = (
        inv_std
        * (
            scaled_grad
            - jnp.mean(scaled_grad, axis=1, keepdims=True)
            - x_hat * jnp.mean(scaled_grad * x_hat, axis=1, keepdims=True)
        )
        + grad_local
    )
    gain_grad, shift_grad, bias_grad = lax.psum(
        (
            jnp.sum(grad_ln_out * x_hat, axis=0),
            jnp.sum(grad_ln_out, axis=0),
            jnp.sum(grad_local, axis=0),
        ),
        ("dp", "tensor"),
    )
    qkv_bias_grad, up_bias_grad = lax.psum((grad_b_qkv, grad_b_up), "dp")
    return (
        output,
        grad_tokens,
        gain_grad,
        shift_grad,
        qkv_summed,
        qkv_bias_grad,
        out_summed,
        up_summed,
        up_bias_grad,
        down_summed,
        bias_grad,
    )


def solution(mesh):
    placed = (
        P(("dp", "tensor"), None),
        P(),
        P(),
        P("dp", None, "tensor"),
        P(None, "tensor"),
        P("tensor", "dp"),
        P("dp", "tensor"),
        P("tensor"),
        P("tensor", "dp"),
        P(),
        P(("dp", "tensor"), None),
    )
    results = (
        P(("dp", "tensor"), None),
        P(("dp", "tensor"), None),
        P(),
        P(),
        P("dp", None, "tensor"),
        P(None, "tensor"),
        P("tensor", "dp"),
        P("dp", "tensor"),
        P("tensor"),
        P("tensor", "dp"),
        P(),
    )
    one_kernel = mesh.shape["dp"] == 8 and mesh.shape["tensor"] == 4
    return jax.shard_map(
        fast_shards if one_kernel else plain_shards,
        mesh=mesh,
        in_specs=placed,
        out_specs=results,
        check_vma=False,
    )
```

profile of v0, /device:TPU:27, one launch (start us, length us, event | category | flops | bytes accessed | tf_op | source)
XLA Modules:
  0.0 372.7 jit_solution(14945394169644088076)
XLA Ops:
  0.6 362.4 %parallel_block.1 = (bf16[256,2048]{1,0:T(8,128)(2,1)}, f32[256,2048]{1,0:T(8,128)}, f32[8,2048]{1,0:T(8,128)}, f32[3,256,1024]{2,1,0:T(8,128)}, bf16[3,4,256,10...) custom-call(bf16[256,2048]{1,0:T(8,128)(2,1)} %tokens.1, ...), custom_call_target="tpu_custom_call" | custom-call | tf_op jit(solution)/shard_map/parallel_block/pallas_call | solution.py:797
  363.1 9.1 %finish.1 = (bf16[256,2048]{1,0:T(8,128)(2,1)}, f32[256,2048]{1,0:T(8,128)}, f32[1,2048]{1,0:T(1,128)}, f32[1,2048]{1,0:T(1,128)}, f32[1,2048]{1,0:T(1,128)}, /*...) custom-call(bf16[256,2048]{1,0:T(8,128)(2,1)} %get-tuple-element.28., ...), custom_call_target="tpu_custom_call" | custom-call | tf_op jit(solution)/shard_map/finish/pallas_call | solution.py:841
where the time goes:
time: 380 us; the launch traced here: 373 us
  Pallas kernels  371 us (98%)
    pallas_call x1, Pallas kernels, fast_shards(): pl.pallas_call(block_kernel, out_shape=(S((T, D), bf16), S((T, D), f32),...  362 us
    pallas_call x1, Pallas kernels, fast_shards(): pl.pallas_call(finish_kernel, out_shape=(S((T, D), bf16), S((T, D), f32),...  9.06 us

commit v1 on v0

--- a/solution.py
+++ b/solution.py
@@ -66,17 +66,18 @@
     "s:Qa", "r:Of", "r:Qh", "hid00", "s:D0e", "r:Qf", "hid01", "near:D011", "s:D0a", "near:D030",
     "proj0", "s:D0c", "att00", "near:D031", "att01", "far:D00", "r:D0h", "r:D0f", "swap:D0",
     "r:D0g", "far:D01", "proj1", "att10", "att11", "near:A30", "core:o11", "core:o01", "cross:o1",
-    "core:o10", "far:A0", "dh00", "near:A10", "dh01", "core:n11", "level:o", "near:U031",
-    "cross:n1", "core:n10", "near:U010", "near:A31", "fin:A", "far:U01", "near:U030", "near:U011",
-    "core:n01", "core:o00", "level:n", "cross:o0", "fin:U0", "near:A11", "far:A1", "cross:n0",
-    "near:D010", "swap:U0", "far:U00", "core:n00", "own:o", "swap:A", "fin:D0", "own:n", "small",
+    "core:o10", "far:A0", "dh00", "near:A10", "dh01", "core:n11", "level:o", "near:U031", "vec",
+    "cross:n1", "core:n10", "near:U010", "near:A31", "v1", "fin:A", "far:U01", "near:U030",
+    "near:U011", "v2", "core:n01", "core:o00", "level:n", "cross:o0", "v3", "fin:U0", "near:A11",
+    "far:A1", "cross:n0", "v4", "near:D010", "swap:U0", "far:U00", "core:n00", "v5", "own:o",
+    "swap:A", "fin:D0", "own:n", "small",
 )
 
 
 def block_kernel(
     tokens, cot, gain, shift, out_bias, wq_in, wo_in, wu_in, wd_in, bq_in, bu_in, cos_t, sin_t,
     o_out, o_gt, o_vec, o_part, ry, rm, rl, rc, rx, rr_lo,
-    XN, G, WU, WD, WQ, WO, ACT, DH, ATT, DP, KS, VS, DK, DV, YS, FF, RING, LD, VEC, SV, SR,
+    XN, G, WU, WD, WQ, WO, ACT, DH, ATT, DP, KS, VS, DK, DV, YS, FF, RING, LD, VEC, SV, SR, SA, SRA,
     ssem, rsem, lsem,
 ):
     T, D = tokens.shape
@@ -673,7 +674,13 @@
     owners("o", 0, rows_out, lambda: weight_ready("D0"), finish_out)
     owners("n", 1, rows_dn, lambda: None, finish_dn)
 
-    def step_small():
+    stage_dev = (to_y, to_hi, to_lo, to_x, to_c)
+    for k in range(5):
+        sends["v%d" % k] = Send(SV, SR.at[k], stage_dev[k])
+        sends["w%d" % k] = Send(SA, SRA.at[k], stage_dev[k])
+    abs_d = {pc: lax.div(abs_block(*pc), R) for pc in pieces}
+
+    def step_vec():
         SV[...] = jnp.zeros_like(SV)
         VEC[6:7, 0 : 3 * H] = jnp.zeros((1, 3 * H), f32)
         VEC[7:8, :] = jnp.zeros((1, D), f32)
@@ -688,23 +695,48 @@
             VEC[7:8, :] += jnp.sum(G[rows, :].astype(f32), axis=0, keepdims=True)
 
         lax.fori_loop(0, T // LN_ROWS, g_body, None)
-        for p, low in pieces:
-            dst = pl.ds(abs_block(p, low), R)
-            SV[0:2, dst] = VEC[4:6, piece_cols(p, low)]
-            SV[2:3, dst] = VEC[7:8, piece_cols(p, low)]
-        SV[3:4, pl.ds(mult(lo * F, F), F)] = VEC[3:4, 0:F]
+        for pc in pieces:
+            at = pl.ds(mult(lax.rem(abs_d[pc], 4) * R, R), R)
+            SV[pl.ds(lax.div(abs_d[pc], 4), 1), at] = VEC[7:8, piece_cols(*pc)]
+        SV[pl.ds(2 + lo, 1), :] = VEC[3:4, 0:F]
         for k in range(3):
             SV[4 + k : 5 + k, pl.ds(mult(lo * H, LANES), H)] = VEC[6:7, k * H : (k + 1) * H]
-        for k, dev in enumerate((to_y, to_hi, to_lo, to_x, to_c)):
-            s = Send(SV, SR.at[k], dev)
-            s.start()
-            s.got()
-            s.done()
-            if k < 3:
-                SV[...] += SR[k]
-            else:
-                SV[0:3, :] += SR[k, 0:3, :]
-        o_vec[...] = SV[...]
+        start("v0")
+
+    def step_v(k):
+        got("v%d" % (k - 1))
+        sends["v%d" % (k - 1)].done()
+        if k <= 3:
+            SV[...] += SR[k - 1]
+        else:
+            SV[0:2, :] += SR[k - 1, 0:2, :]
+        if k < 5:
+            start("v%d" % k)
+        else:
+            o_vec[2:3, 0:half_d] = SV[0:1, :]
+            o_vec[2:3, half_d:] = SV[1:2, :]
+            o_vec[3:4, 0:half_d] = SV[2:3, :]
+            o_vec[3:4, half_d:] = SV[3:4, :]
+            o_vec[4:7, 0:half_d] = SV[4:7, :]
+
+    steps["vec"] = step_vec
+    for k in range(1, 6):
+        steps["v%d" % k] = functools.partial(step_v, k)
+
+    def step_small():
+        quarter = D // 4
+        for row_, base in ((4, 0), (5, 4)):
+            for pc in pieces:
+                at = pl.ds(mult(lax.rem(abs_d[pc], 2) * R, R), R)
+                SA[pl.ds(base + lax.div(abs_d[pc], 2), 1), at] = VEC[row_ : row_ + 1, piece_cols(*pc)]
+        for k in range(5):
+            start("w%d" % k)
+            got("w%d" % k)
+            sends["w%d" % k].done()
+            SA[...] += SRA[k]
+        for i in range(4):
+            o_vec[0:1, i * quarter : (i + 1) * quarter] = SA[i : i + 1, :]
+            o_vec[1:2, i * quarter : (i + 1) * quarter] = SA[4 + i : 5 + i, :]
 
     steps["small"] = step_small
 
@@ -712,6 +744,7 @@
     for dev in partners:
         pl.semaphore_signal(barrier, inc=1, device_id=dev, device_id_type=pl.DeviceIdType.MESH)
     pl.semaphore_wait(barrier, len(partners))
+    o_vec[...] = jnp.zeros_like(o_vec)
     for name in ORDER:
         steps[name]()
     ff_free(0, 1)
@@ -823,10 +856,12 @@
             pltpu.VMEM((3, T, D), bf16),
             pltpu.VMEM((2, T, D), bf16),
             pltpu.VMEM((8, D), f32),
-            pltpu.VMEM((8, D), f32),
-            pltpu.VMEM((5, 8, D), f32),
-            pltpu.SemaphoreType.DMA((90,)),
-            pltpu.SemaphoreType.DMA((90,)),
+            pltpu.VMEM((8, D // 2), f32),
+            pltpu.VMEM((5, 8, D // 2), f32),
+            pltpu.VMEM((8, D // 4), f32),
+            pltpu.VMEM((5, 8, D // 4), f32),
+            pltpu.SemaphoreType.DMA((96,)),
+            pltpu.SemaphoreType.DMA((96,)),
             pltpu.SemaphoreType.DMA((110,)),
         ],
         compiler_params=pltpu.CompilerParams(

time: 380 us -> 378 us (level)
  no operation moved by 1% of the time
where the time goes in v1:
time: 378 us; the launch traced here: 372 us
  Pallas kernels  370 us (98%)
    pallas_call x1, Pallas kernels, fast_shards(): pl.pallas_call(block_kernel, out_shape=(S((T, D), bf16), S((T, D), f32),...  361 us
    pallas_call x1, Pallas kernels, fast_shards(): pl.pallas_call(finish_kernel, out_shape=(S((T, D), bf16), S((T, D), f32),...  9.06 us

profile of v1, /device:TPU:27, one launch (start us, length us, event | category | flops | bytes accessed | tf_op | source)
XLA Modules:
  0.0 371.6 jit_solution(8539343588853326674)
XLA Ops:
  0.6 361.4 %parallel_block.1 = (bf16[256,2048]{1,0:T(8,128)(2,1)}, f32[256,2048]{1,0:T(8,128)}, f32[8,2048]{1,0:T(8,128)}, f32[3,256,1024]{2,1,0:T(8,128)}, bf16[3,4,256,10...) custom-call(bf16[256,2048]{1,0:T(8,128)(2,1)} %tokens.1, ...), custom_call_target="tpu_custom_call" | custom-call | tf_op jit(solution)/shard_map/parallel_block/pallas_call | solution.py:830
  362.0 9.1 %finish.1 = (bf16[256,2048]{1,0:T(8,128)(2,1)}, f32[256,2048]{1,0:T(8,128)}, f32[1,2048]{1,0:T(1,128)}, f32[1,2048]{1,0:T(1,128)}, f32[1,2048]{1,0:T(1,128)}, /*...) custom-call(bf16[256,2048]{1,0:T(8,128)(2,1)} %get-tuple-element.28., ...), custom_call_target="tpu_custom_call" | custom-call | tf_op jit(solution)/shard_map/finish/pallas_call | solution.py:876

commit v2 on v1

--- a/solution.py
+++ b/solution.py
@@ -23,7 +23,7 @@
 
 GELU_A = math.sqrt(2.0 / math.pi)
 GELU_B = 0.044715
-CHUNK = 512
+CHUNK = 1024
 Q_BLOCK = 128
 LANES = 128
 

time: 378 us -> 376 us (level)
  no operation moved by 1% of the time
where the time goes in v2:
time: 376 us; the launch traced here: 370 us
  Pallas kernels  369 us (98%)
    pallas_call x1, Pallas kernels, fast_shards(): pl.pallas_call(block_kernel, out_shape=(S((T, D), bf16), S((T, D), f32),...  360 us
    pallas_call x1, Pallas kernels, fast_shards(): pl.pallas_call(finish_kernel, out_shape=(S((T, D), bf16), S((T, D), f32),...  9.06 us

profile of v2, /device:TPU:27, one launch (start us, length us, event | category | flops | bytes accessed | tf_op | source)
XLA Modules:
  0.0 370.3 jit_solution(178353704985743248)
XLA Ops:
  0.6 360.3 %parallel_block.1 = (bf16[256,2048]{1,0:T(8,128)(2,1)}, f32[256,2048]{1,0:T(8,128)}, f32[8,2048]{1,0:T(8,128)}, f32[3,256,1024]{2,1,0:T(8,128)}, bf16[3,4,256,10...) custom-call(bf16[256,2048]{1,0:T(8,128)(2,1)} %tokens.1, ...), custom_call_target="tpu_custom_call" | custom-call | tf_op jit(solution)/shard_map/parallel_block/pallas_call | solution.py:830
  361.0 9.1 %finish.1 = (bf16[256,2048]{1,0:T(8,128)(2,1)}, f32[256,2048]{1,0:T(8,128)}, f32[1,2048]{1,0:T(1,128)}, f32[1,2048]{1,0:T(1,128)}, f32[1,2048]{1,0:T(1,128)}, /*...) custom-call(bf16[256,2048]{1,0:T(8,128)(2,1)} %get-tuple-element.28., ...), custom_call_target="tpu_custom_call" | custom-call | tf_op jit(solution)/shard_map/finish/pallas_call | solution.py:876
